TPU v7x, 32 devices: a whole 2x2x4 slice. The times are simulated.
32 devices in a mesh: groups: 2 (over y), hid: 4 (over z), wid: 4 (over x, core).
Axes of the slice: x: 2, y: 2, z: 4, core: 2. Of those that a mesh axis runs over, the one named last changes fastest.
Arguments:
- activations: bfloat16 [512, 8192], P(('groups', 'hid'), 'wid'), parts along dimension 0, may hold values from -50 to 50, as said below
- norm_gain: float32 [8192], P('wid'), may hold values from 0.1 to 1.9
- gate_weight: bfloat16 [8192, 28672], P('wid', 'hid'), may hold values from -0.0625 to 0.0625
- up_weight: bfloat16 [8192, 28672], P('wid', 'hid'), may hold values from -0.0625 to 0.0625
- down_weight: bfloat16 [28672, 8192], P('hid', 'wid'), may hold values from -0.0625 to 0.0625
Outputs:
- final_rows: bfloat16 [512, 8192], P(('groups', 'hid'), 'wid'), parts along dimension 0
There are 2 independent parts, one for each index of `groups`. A program takes and returns all parts, laid end to end along the dimension named above; an argument that names none is the same for every part. Nothing has to cross between parts.
Inputs may be any that keep to these rules, and one draw needn't show every extreme that they name: real-valued activations.
All inputs are finite; a program needn't handle non-finite values.
Results may differ from a plain program's by a relative error of at most 0.019.
Values may be sent and summed in bfloat16 or wider, within the bound.
A program may use at most 192 MiB of HBM per device.

v0:
```python
import jax
import jax.numpy as jnp
from jax import lax
from jax.sharding import PartitionSpec as P

D = 8192


def normed(values, norm_gain):
    wide = values.astype(jnp.float32)
    partial_sq = jnp.sum(wide * wide, axis=1)
    total_sq = lax.psum(partial_sq, "wid")
    factor = lax.rsqrt(total_sq / D + 1e-05)
    return (wide * factor[:, None] * norm_gain[None, :]).astype(jnp.bfloat16)


def project_local(inputs, gate_weight, up_weight):
    gate_part = jnp.dot(inputs, gate_weight, preferred_element_type=jnp.float32)
    up_part = jnp.dot(inputs, up_weight, preferred_element_type=jnp.float32)
    return jnp.stack([gate_part, up_part]).astype(jnp.bfloat16).astype(jnp.float32)


def combine_hidden(partials):
    shared = lax.psum_scatter(
        partials.astype(jnp.bfloat16), "wid", scatter_dimension=2, tiled=True
    ).astype(jnp.float32)
    hidden_share = (jax.nn.silu(shared[0]) * shared[1]).astype(jnp.bfloat16)
    return lax.all_gather(hidden_share, "wid", axis=1, tiled=True)


def hidden_from_share(normed_share, gate_weight, up_weight):
    partials = project_local(
        lax.all_gather(normed_share, "hid", axis=0, tiled=True), gate_weight, up_weight
    )
    return combine_hidden(partials)


def down_share(hidden, down_weight):
    return lax.psum_scatter(
        jnp.dot(hidden, down_weight, preferred_element_type=jnp.float32).astype(jnp.bfloat16),
        "hid",
        scatter_dimension=0,
        tiled=True,
    ).astype(jnp.float32)


def body(activations, norm_gain, gate_weight, up_weight, down_weight):
    first_hidden = hidden_from_share(normed(activations, norm_gain), gate_weight, up_weight)
    first_own = (activations.astype(jnp.float32) + down_share(first_hidden, down_weight)).astype(
        jnp.bfloat16
    )
    second_hidden = hidden_from_share(normed(first_own, norm_gain), gate_weight, up_weight)
    second_branch = down_share(second_hidden, down_weight)
    return (first_own.astype(jnp.float32) + second_branch).astype(jnp.bfloat16)


def solution(mesh):
    placed = (
        P(("groups", "hid"), "wid"),
        P("wid"),
        P("wid", "hid"),
        P("wid", "hid"),
        P("hid", "wid"),
    )
    return jax.shard_map(
        body, mesh=mesh, in_specs=placed, out_specs=P(("groups", "hid"), "wid"), check_vma=False
    )
```

profile of v0, /device:TPU:12, one launch (start us, length us, event | category | flops | bytes accessed | tf_op | source)
XLA Modules:
  0.0 440.9 jit_solution(15490147069975802724)
XLA Ops:
  6.5 0.0 all-gather.5.cloned.1.call-start
  6.5 1.1 fusion.8
  7.6 6.9 %psum.14 = f32[64]{0:T(128)S(1)} all-reduce(f32[64]{0:T(128)S(1)} %fusion.8), channel_id=1, replica_groups=mesh['groups'=2,'hid'=4,'wid'=4] {'wid'}, use_global_device_ids=true, to_apply=%region_1.0 | all-reduce | flops 64 | bytes 512 | tf_op jit(solution)/shard_map/psum | solution.py:12
  14.5 1.8 fusion.10
  16.3 0.0 all-gather.5.cloned.1.call-update
  16.4 0.0 reduce-scatter.5.cloned.1.call-start
  16.4 28.2 %all-gather.5.cloned.1.call-done = bf16[256,2048]{1,0:T(8,128)(2,1)} async-done(((bf16[64,2048]{1,0:T(8,128)(2,1)}), bf16[256,2048]{1,0:T(8,128)(2,1)}) %all-gather.5.cloned.1.call-update) | async-done | bytes 1048592 | tf_op jit(solution)/shard_map/all_gather | solution.py:33
  44.6 17.6 %fusion.1 = bf16[1,256,7168]{2,1,0:T(8,128)(2,1)S(1)} fusion(bf16[256,2048]{1,0:T(8,128)(2,1)} %all-gather.5.cloned.1.call-done, bf16[2048,7168]{1,0:T(8,128)(2,1)} %param.8), kind=kOutput, calls=%fused_computation.5 | convolution fusion | flops 7518027776 | bytes 34078720 | tf_op jit(solution)/shard_map/dot_general | solution.py:19
  62.2 0.0 copy-done.3
  62.2 13.3 %fusion = bf16[1,256,7168]{2,1,0:T(8,128)(2,1)S(1)} fusion(bf16[256,2048]{1,0:T(8,128)(2,1)S(1)} %copy-done.3, bf16[2048,7168]{1,0:T(8,128)(2,1)} %param.7), kind=kOutput, calls=%fused_computation.4 | convolution fusion | flops 7518027776 | bytes 34078720 | tf_op jit(solution)/shard_map/dot_general | solution.py:18
  75.5 3.6 pad_maximum_fusion
  79.1 0.0 reduce-scatter.5.cloned.1.call-update
  79.1 0.0 all-gather.7.cloned.1.call-start
  79.2 65.1 %reduce-scatter.5.cloned.1.call-done = bf16[2,256,1792]{2,1,0:T(8,128)(2,1)} async-done(((bf16[2,256,7168]{2,1,0:T(8,128)(2,1)}), bf16[2,256,1792]{2,1,0:T(8,128)(2,1)}) %reduce-scatter.5.cloned.1.call-update) | async-done | bytes 1835024 | tf_op jit(solution)/shard_map/reduce_scatter | solution.py:24
  144.3 1.8 convert_element_type.52
  146.0 1.5 fusion.7
  147.5 0.0 all-gather.7.cloned.1.call-update
  147.5 0.0 copy-start
  147.5 0.0 copy-start.2
  147.5 0.0 reduce-scatter.7.cloned.1.call-start
  147.6 31.6 %all-gather.7.cloned.1.call-done = bf16[256,7168]{1,0:T(8,128)(2,1)} async-done(((bf16[256,1792]{1,0:T(8,128)(2,1)}), bf16[256,7168]{1,0:T(8,128)(2,1)}) %all-gather.7.cloned.1.call-update) | async-done | bytes 3670032 | tf_op jit(solution)/shard_map/all_gather | solution.py:28
  179.2 15.2 %convolution_convert_fusion.5 = bf16[256,2048]{1,0:T(8,128)(2,1)} fusion(bf16[256,7168]{1,0:T(8,128)(2,1)} %all-gather.7.cloned.1.call-done, bf16[7168,2048]{1,0:T(8,128)(2,1)} %param.9), kind=kOutput, calls=%fused_computation.11 | convolution fusion | flops 7516717056 | bytes 34078720 | tf_op jit(solution)/shard_map/dot_general | solution.py:40
  194.4 0.0 reduce-scatter.7.cloned.1.call-update
  194.4 0.0 all-gather.9.cloned.1.call-start
  194.4 25.2 %reduce-scatter.7.cloned.1.call-done = bf16[64,2048]{1,0:T(8,128)(2,1)} async-done(((bf16[256,2048]{1,0:T(8,128)(2,1)}), bf16[64,2048]{1,0:T(8,128)(2,1)}) %reduce-scatter.7.cloned.1.call-update) | async-done | bytes 262160 | tf_op jit(solution)/shard_map/reduce_scatter | solution.py:39
  219.6 0.0 copy-done
  219.6 1.1 fusion.12
  220.8 6.8 %psum.15 = f32[64]{0:T(128)S(1)} all-reduce(f32[64]{0:T(128)S(1)} %fusion.12), channel_id=1, replica_groups=mesh['groups'=2,'hid'=4,'wid'=4] {'wid'}, use_global_device_ids=true, to_apply=%region_5.6 | all-reduce | flops 64 | bytes 512 | tf_op jit(solution)/shard_map/psum | solution.py:12
  227.6 1.8 fusion.14
  229.4 0.0 all-gather.9.cloned.1.call-update
  229.4 0.2 reduce-scatter.9.cloned.1.call-start
  229.6 27.6 %all-gather.9.cloned.1.call-done = bf16[256,2048]{1,0:T(8,128)(2,1)} async-done(((bf16[64,2048]{1,0:T(8,128)(2,1)}), bf16[256,2048]{1,0:T(8,128)(2,1)}) %all-gather.9.cloned.1.call-update) | async-done | bytes 1048592 | tf_op jit(solution)/shard_map/all_gather | solution.py:33
  257.3 17.6 %fusion.3 = bf16[1,256,7168]{2,1,0:T(8,128)(2,1)S(1)} fusion(bf16[256,2048]{1,0:T(8,128)(2,1)} %all-gather.9.cloned.1.call-done, bf16[2048,7168]{1,0:T(8,128)(2,1)} %param.8), kind=kOutput, calls=%fused_computation.7 | convolution fusion | flops 7518027776 | bytes 34078720 | tf_op jit(solution)/shard_map/dot_general | solution.py:19
  274.9 13.3 %fusion.2 = bf16[1,256,7168]{2,1,0:T(8,128)(2,1)S(1)} fusion(bf16[256,2048]{1,0:T(8,128)(2,1)S(1)} %copy-done.4, bf16[2048,7168]{1,0:T(8,128)(2,1)} %param.7), kind=kOutput, calls=%fused_computation.6 | convolution fusion | flops 7518027776 | bytes 34078720 | tf_op jit(solution)/shard_map/dot_general | solution.py:18
  288.2 3.6 pad_maximum_fusion.1
  291.8 0.0 reduce-scatter.9.cloned.1.call-update
  291.8 0.0 all-gather.11.cloned.1.call-start
  291.9 65.1 %reduce-scatter.9.cloned.1.call-done = bf16[2,256,1792]{2,1,0:T(8,128)(2,1)} async-done(((bf16[2,256,7168]{2,1,0:T(8,128)(2,1)}), bf16[2,256,1792]{2,1,0:T(8,128)(2,1)}) %reduce-scatter.9.cloned.1.call-update) | async-done | bytes 1835024 | tf_op jit(solution)/shard_map/reduce_scatter | solution.py:24
  356.9 1.8 convert_element_type.59
  358.7 1.5 fusion.5
  360.2 0.0 all-gather.11.cloned.1.call-update
  360.2 0.0 reduce-scatter.11.cloned.1.call-start
  360.3 31.6 %all-gather.11.cloned.1.call-done = bf16[256,7168]{1,0:T(8,128)(2,1)} async-done(((bf16[256,1792]{1,0:T(8,128)(2,1)}), bf16[256,7168]{1,0:T(8,128)(2,1)}) %all-gather.11.cloned.1.call-update) | async-done | bytes 3670032 | tf_op jit(solution)/shard_map/all_gather | solution.py:28
  391.9 15.2 %convolution_convert_fusion.4 = bf16[256,2048]{1,0:T(8,128)(2,1)} fusion(bf16[256,7168]{1,0:T(8,128)(2,1)} %all-gather.11.cloned.1.call-done, bf16[7168,2048]{1,0:T(8,128)(2,1)} %param.9), kind=kOutput, calls=%fused_computation.10 | convolution fusion | flops 7516717056 | bytes 34078720 | tf_op jit(solution)/shard_map/dot_general | solution.py:40
  407.0 0.0 reduce-scatter.11.cloned.1.call-update
  407.1 25.2 %reduce-scatter.11.cloned.1.call-done = bf16[64,2048]{1,0:T(8,128)(2,1)} async-done(((bf16[256,2048]{1,0:T(8,128)(2,1)}), bf16[64,2048]{1,0:T(8,128)(2,1)}) %reduce-scatter.11.cloned.1.call-update) | async-done | bytes 262160 | tf_op jit(solution)/shard_map/reduce_scatter | solution.py:39
  432.3 0.0 copy-done.1
  432.3 1.7 fusion.15
  (7 shorter events, 0.0 us)
Async XLA Ops:
  6.5 38.1 %all-gather.5.cloned.1.call-start = ((), (), s32[]{:S(2)}) async-start(), calls=%async_computation.4 | async-start | bytes 1310720 | tf_op jit(solution)/shard_map/all_gather | solution.py:33
  16.4 127.9 %reduce-scatter.5.cloned.1.call-start = ((), (), s32[]{:S(2)}) async-start(), calls=%async_computation.5 | async-start | bytes 9175040 | tf_op jit(solution)/shard_map/reduce_scatter | solution.py:24
  44.6 17.6 %copy-start.3 = (bf16[256,2048]{1,0:T(8,128)(2,1)S(1)}, bf16[256,2048]{1,0:T(8,128)(2,1)}, u32[]{:S(2)}) copy-start(bf16[256,2048]{1,0:T(8,128)(2,1)} %all-gather.5.cloned.1.call-done) | copy-start | bytes 3145732
  79.1 100.0 %all-gather.7.cloned.1.call-start = ((), (), s32[]{:S(2)}) async-start(), calls=%async_computation.6 | async-start | bytes 4587520 | tf_op jit(solution)/shard_map/all_gather | solution.py:28
  147.5 72.1 %copy-start = (bf16[64,2048]{1,0:T(8,128)(2,1)S(1)}, bf16[64,2048]{1,0:T(8,128)(2,1)}, u32[]{:S(2)}) copy-start(bf16[64,2048]{1,0:T(8,128)(2,1)} %param.5) | copy-start | bytes 786436
  147.5 80.1 %copy-start.2 = (f32[2048]{0:T(1024)S(1)}, f32[2048]{0:T(1024)}, u32[]{:S(2)}) copy-start(f32[2048]{0:T(1024)} %param.6) | copy-start | bytes 24580
  147.5 72.1 %reduce-scatter.7.cloned.1.call-start = ((), (), s32[]{:S(2)}) async-start(), calls=%async_computation.7 | async-start | bytes 1310720 | tf_op jit(solution)/shard_map/reduce_scatter | solution.py:39
  194.4 62.9 %all-gather.9.cloned.1.call-start = ((), (), s32[]{:S(2)}) async-start(), calls=%async_computation.8 | async-start | bytes 1310720 | tf_op jit(solution)/shard_map/all_gather | solution.py:33
  229.4 127.5 %reduce-scatter.9.cloned.1.call-start = ((), (), s32[]{:S(2)}) async-start(), calls=%async_computation.9 | async-start | bytes 9175040 | tf_op jit(solution)/shard_map/reduce_scatter | solution.py:24
  257.3 17.6 %copy-start.4 = (bf16[256,2048]{1,0:T(8,128)(2,1)S(1)}, bf16[256,2048]{1,0:T(8,128)(2,1)}, u32[]{:S(2)}) copy-start(bf16[256,2048]{1,0:T(8,128)(2,1)} %all-gather.9.cloned.1.call-done) | copy-start | bytes 3145732
  291.8 100.0 %all-gather.11.cloned.1.call-start = ((), (), s32[]{:S(2)}) async-start(), calls=%async_computation.10 | async-start | bytes 4587520 | tf_op jit(solution)/shard_map/all_gather | solution.py:28
  360.2 72.1 %copy-start.1 = (bf16[64,2048]{1,0:T(8,128)(2,1)S(1)}, bf16[64,2048]{1,0:T(8,128)(2,1)}, u32[]{:S(2)}) copy-start(bf16[64,2048]{1,0:T(8,128)(2,1)} %reduce-scatter.7.cloned.1.call-done) | copy-start | bytes 786436
  360.2 72.1 %reduce-scatter.11.cloned.1.call-start = ((), (), s32[]{:S(2)}) async-start(), calls=%async_computation.11 | async-start | bytes 1310720 | tf_op jit(solution)/shard_map/reduce_scatter | solution.py:39
Sparse Core Ops, SparseCore 0:
  16.5 28.0 all-gather.4
  79.2 64.9 reduce-scatter.4
  147.6 31.5 all-gather.6
  194.5 25.0 reduce-scatter.6
  229.5 27.7 all-gather.8
  291.9 64.9 reduce-scatter.8
  360.3 31.5 all-gather.10
  407.2 25.0 reduce-scatter.10
where the time goes:
time: 445 us; the launch traced here: 441 us
  waiting for transfers between devices  300 us (67%)
  matrix products  92.2 us (21%)
  other arithmetic  21.1 us (5%)
  blocking collectives  13.7 us (3%)
  between operations  13.6 us (3%)
    reduce_scatter x2, waiting for transfers between devices, combine_hidden(): lax.psum_scatter(partials.astype(jnp.bfloat16), 'wid', scatter_dimension=...  130 us
    all_gather x2, waiting for transfers between devices, combine_hidden(): return lax.all_gather(hidden_share, 'wid', axis=1, tiled=True)  63.2 us
    all_gather x2, waiting for transfers between devices, hidden_from_share(): lax.all_gather(normed_share, 'hid', axis=0, tiled=True)  55.8 us
    reduce_scatter x2, waiting for transfers between devices, down_share(): lax.psum_scatter(jnp.dot(hidden, down_weight, preferred_element_type=jnp....  50.4 us
    dot_general x2, matrix products, project_local(): up_part = jnp.dot(inputs, up_weight, preferred_element_type=jnp.float32)  35.2 us
    dot_general x2, matrix products, down_share(): jnp.dot(hidden, down_weight, preferred_element_type=jnp.float32)  30.4 us
    dot_general x2, matrix products, project_local(): gate_part = jnp.dot(inputs, gate_weight, preferred_element_type=jnp.float32)  26.7 us
    psum x2, blocking collectives, normed(): total_sq = lax.psum(partial_sq, 'wid')  13.7 us
  transfers between devices with their start and end apart: 8, of which 8 were waited for; matrix products, arithmetic and copies ran while one was open for 0% of the time, Pallas kernels for 0%

commit v1 on v0

--- a/solution.py
+++ b/solution.py
@@ -1,16 +1,25 @@
+import functools
+
 import jax
 import jax.numpy as jnp
 from jax import lax
+from jax.experimental import pallas as pl
+from jax.experimental.pallas import tpu as pltpu
 from jax.sharding import PartitionSpec as P
 
 D = 8192
+EPS = 1e-05
+UNITS = 512
+LAG2, LAG3, LAG4, LAG5 = 1, 3, 5, 6
+LAG_ROWS, LAG_NORM = 4, 2
+RING = 8
 
 
 def normed(values, norm_gain):
     wide = values.astype(jnp.float32)
     partial_sq = jnp.sum(wide * wide, axis=1)
     total_sq = lax.psum(partial_sq, "wid")
-    factor = lax.rsqrt(total_sq / D + 1e-05)
+    factor = lax.rsqrt(total_sq / D + EPS)
     return (wide * factor[:, None] * norm_gain[None, :]).astype(jnp.bfloat16)
 
 
@@ -44,7 +53,7 @@
     ).astype(jnp.float32)
 
 
-def body(activations, norm_gain, gate_weight, up_weight, down_weight):
+def plain_body(activations, norm_gain, gate_weight, up_weight, down_weight):
     first_hidden = hidden_from_share(normed(activations, norm_gain), gate_weight, up_weight)
     first_own = (activations.astype(jnp.float32) + down_share(first_hidden, down_weight)).astype(
         jnp.bfloat16
@@ -52,6 +61,255 @@
     second_hidden = hidden_from_share(normed(first_own, norm_gain), gate_weight, up_weight)
     second_branch = down_share(second_hidden, down_weight)
     return (first_own.astype(jnp.float32) + second_branch).astype(jnp.bfloat16)
+
+
+def kernel(
+    chunks, x_ref, gain_ref, wg_hbm, wu_hbm, wd_hbm, out_ref,
+    wgu, wd, rows, acts, part, recv_a, send_b, recv_b, hidden, acc, rs_send, rs_recv,
+    stat_send, stat_recv,
+    w_sem, wd_sem, sa_sem, ra_sem, sb_sem, rb_sem, sh_sem, rh_sem, sg_sem, rg_sem,
+    srs_sem, rrs_sem, sag_sem, rag_sem, sst_sem, rst_sem,
+):
+    total = 4 * chunks
+    h = lax.axis_index("hid")
+    w = lax.axis_index("wid")
+    chip, core = lax.div(w, 2), lax.rem(w, 2)
+    other_core = 2 * chip + (1 - core)
+    other_chip = 2 * (1 - chip) + core
+    half_rows = rows.shape[1]
+    width = rows.shape[2]
+
+    def remote(src, dst, send, recv, axis, peer):
+        return pltpu.make_async_remote_copy(
+            src_ref=src, dst_ref=dst, send_sem=send, recv_sem=recv,
+            device_id={axis: peer}, device_id_type=pl.DeviceIdType.MESH,
+        )
+
+    barrier = pltpu.get_barrier_semaphore()
+    for d in (1, 2, 3):
+        pl.semaphore_signal(barrier, inc=1, device_id={"wid": lax.rem(w + d, 4)},
+                            device_id_type=pl.DeviceIdType.MESH)
+        pl.semaphore_signal(barrier, inc=1, device_id={"hid": lax.rem(h + d, 4)},
+                            device_id_type=pl.DeviceIdType.MESH)
+
+    def weight_copies(g):
+        columns = pl.ds(pl.multiple_of(lax.rem(g, chunks) * UNITS, UNITS), UNITS)
+        slot = lax.rem(g, 2)
+        return (
+            pltpu.make_async_copy(wg_hbm.at[:, columns], wgu.at[slot, 0], w_sem.at[slot, 0]),
+            pltpu.make_async_copy(wu_hbm.at[:, columns], wgu.at[slot, 1], w_sem.at[slot, 1]),
+        )
+
+    def down_copy(c):
+        span = pl.ds(pl.multiple_of(c * UNITS, UNITS), UNITS)
+        return pltpu.make_async_copy(wd_hbm.at[span, :], wd.at[c], wd_sem.at[c])
+
+    def stat_copy(q, d):
+        return remote(stat_send.at[q], stat_recv.at[q, d - 1], sst_sem.at[q, d - 1],
+                      rst_sem.at[q, d - 1], "wid", lax.rem(w + d, 4))
+
+    def gather_copy(half, d):
+        return remote(acts.at[half, h], acts.at[half, h], sag_sem.at[half, d - 1],
+                      rag_sem.at[half, d - 1], "hid", lax.rem(h + d, 4))
+
+    def place(owner):
+        return lax.rem(owner, 2) * 2 + lax.div(owner, 2)
+
+    def scatter_copy(half, d):
+        owner = lax.rem(h + d, 4)
+        return remote(rs_send.at[half, place(owner)], rs_recv.at[half, d - 1],
+                      srs_sem.at[half, d - 1], rrs_sem.at[half, d - 1], "hid", owner)
+
+    def send_stats(q, wide):
+        sums = jnp.sum(wide * wide, axis=1, keepdims=True)
+        stat_send[q] = jnp.broadcast_to(sums, (half_rows, 128))
+        for d in (1, 2, 3):
+            stat_copy(q, d).start()
+
+    def norm_rows(q, half):
+        for d in (1, 2, 3):
+            stat_copy(q, d).wait()
+        sums = (stat_send[q] + stat_recv[q, 0]) + (stat_recv[q, 1] + stat_recv[q, 2])
+        factor = lax.rsqrt(sums[:, :1] / D + EPS)
+        wide = rows[half].astype(jnp.float32)
+        acts[half, h] = (wide * factor * gain_ref[...]).astype(jnp.bfloat16)
+        for d in (1, 2, 3):
+            gather_copy(half, d).start()
+
+    for copy in weight_copies(0):
+        copy.start()
+    for half in (0, 1):
+        rows[half] = x_ref[half * half_rows:(half + 1) * half_rows]
+    pl.semaphore_wait(barrier, 6)
+    for half in (0, 1):
+        send_stats(half, rows[half].astype(jnp.float32))
+    for half in (0, 1):
+        norm_rows(half, half)
+
+    def stage_copies(cc):
+        ring, both = lax.rem(cc, RING), lax.rem(cc, 2 * chunks)
+        half, c = lax.div(both, chunks), lax.rem(both, chunks)
+        a = remote(part.at[ring, 1 - core], recv_a.at[half, c], sa_sem.at[ring],
+                   ra_sem.at[both], "wid", other_core)
+        b = remote(send_b.at[ring], recv_b.at[half, c], sb_sem.at[ring],
+                   rb_sem.at[both], "wid", other_chip)
+        hid = remote(hidden.at[half, c, core, chip], hidden.at[half, c, core, chip],
+                     sh_sem.at[ring], rh_sem.at[both], "wid", other_chip)
+        pair = remote(hidden.at[half, c, core], hidden.at[half, c, core],
+                      sg_sem.at[ring], rg_sem.at[both], "wid", other_core)
+        return ring, half, c, a, b, hid, pair
+
+    def body(g, carry):
+        @pl.when(g < total)
+        def _():
+            ring, half, c, a, *_ = stage_copies(g)
+
+            @pl.when(g + 1 < total)
+            def _():
+                for copy in weight_copies(g + 1):
+                    copy.start()
+
+            @pl.when(g < chunks)
+            def _():
+                down_copy(c).start()
+
+            @pl.when(c == 0)
+            def _():
+                for d in (1, 2, 3):
+                    gather_copy(half, d).wait()
+
+            slot = lax.rem(g, 2)
+            for copy in weight_copies(g):
+                copy.wait()
+            left = acts[half].reshape(4 * half_rows, width)
+            for gu in (0, 1):
+                product = jnp.dot(left, wgu[slot, gu], preferred_element_type=jnp.float32)
+                product = product.astype(jnp.bfloat16)
+                for b in range(4):
+                    part[ring, b % 2, b // 2, gu] = product[b * half_rows:(b + 1) * half_rows]
+            a.start()
+
+        @pl.when((g >= LAG2) & (g < total + LAG2))
+        def _():
+            ring, half, c, a, b, *_ = stage_copies(g - LAG2)
+            a.wait()
+            send_b[ring] = (
+                part[ring, core, 1 - chip].astype(jnp.float32)
+                + recv_a[half, c, 1 - chip].astype(jnp.float32)
+            ).astype(jnp.bfloat16)
+            b.start()
+
+        @pl.when((g >= LAG3) & (g < total + LAG3))
+        def _():
+            ring, half, c, a, b, hid, _ = stage_copies(g - LAG3)
+            b.wait()
+            sums = (
+                part[ring, core, chip].astype(jnp.float32)
+                + recv_a[half, c, chip].astype(jnp.float32)
+            ) + recv_b[half, c].astype(jnp.float32)
+            gate, up = sums[0], sums[1]
+            hidden[half, c, core, chip] = (gate / (1.0 + jnp.exp(-gate)) * up).astype(jnp.bfloat16)
+            hid.start()
+
+        @pl.when((g >= LAG4) & (g < total + LAG4))
+        def _():
+            *_, hid, pair = stage_copies(g - LAG4)
+            hid.wait()
+            pair.start()
+
+        @pl.when((g >= LAG5) & (g < total + LAG5))
+        def _():
+            cc = g - LAG5
+            ring, half, c, *_, pair = stage_copies(cc)
+
+            @pl.when(cc < chunks)
+            def _():
+                down_copy(c).wait()
+
+            @pl.when(c == 0)
+            def _():
+                acc[...] = jnp.zeros_like(acc)
+
+            pair.wait()
+            left = hidden[half, c].reshape(4 * half_rows, UNITS)
+            for n in range(0, width, 512):
+                acc[:, n:n + 512] += jnp.dot(
+                    left, wd[c, :, n:n + 512], preferred_element_type=jnp.float32
+                )
+
+            @pl.when(c == chunks - 1)
+            def _():
+                rs_send[half] = acc[...].astype(jnp.bfloat16).reshape(4, half_rows, width)
+                for d in (1, 2, 3):
+                    scatter_copy(half, d).start()
+
+        for q in range(4):
+            half = q % 2
+            at = q * chunks + chunks - 1 + LAG5 + LAG_ROWS
+
+            @pl.when(g == at)
+            def _():
+                for d in (1, 2, 3):
+                    scatter_copy(half, d).wait()
+                branch = rs_send[half, place(h)].astype(jnp.float32)
+                for d in (1, 2, 3):
+                    branch = branch + rs_recv[half, d - 1].astype(jnp.float32)
+                new = (rows[half].astype(jnp.float32) + branch).astype(jnp.bfloat16)
+                if q < 2:
+                    rows[half] = new
+                    send_stats(q + 2, new.astype(jnp.float32))
+                else:
+                    out_ref[half * half_rows:(half + 1) * half_rows] = new
+
+            if q < 2:
+                @pl.when(g == at + LAG_NORM)
+                def _():
+                    norm_rows(q + 2, half)
+
+        return carry
+
+    lax.fori_loop(0, total + LAG5 + LAG_ROWS, body, 0)
+
+
+def kernel_body(activations, norm_gain, gate_weight, up_weight, down_weight):
+    own_rows, width = activations.shape
+    chunks = gate_weight.shape[1] // UNITS
+    hr = own_rows // 2
+    bf, f32, dma = jnp.bfloat16, jnp.float32, pltpu.SemaphoreType.DMA
+    vmem, hbm = pl.BlockSpec(memory_space=pltpu.VMEM), pl.BlockSpec(memory_space=pl.ANY)
+    flops = 2 * 2 * 3 * 4 * own_rows * width * gate_weight.shape[1]
+    return pl.pallas_call(
+        functools.partial(kernel, chunks),
+        out_shape=jax.ShapeDtypeStruct((own_rows, width), bf),
+        in_specs=[vmem, vmem, hbm, hbm, hbm],
+        out_specs=vmem,
+        scratch_shapes=[
+            pltpu.VMEM((2, 2, width, UNITS), bf),
+            pltpu.VMEM((chunks, UNITS, width), bf),
+            pltpu.VMEM((2, hr, width), bf),
+            pltpu.VMEM((2, 4, hr, width), bf),
+            pltpu.VMEM((RING, 2, 2, 2, hr, UNITS), bf),
+            pltpu.VMEM((2, chunks, 2, 2, hr, UNITS), bf),
+            pltpu.VMEM((RING, 2, hr, UNITS), bf),
+            pltpu.VMEM((2, chunks, 2, hr, UNITS), bf),
+            pltpu.VMEM((2, chunks, 2, 2, hr, UNITS), bf),
+            pltpu.VMEM((4 * hr, width), f32),
+            pltpu.VMEM((2, 4, hr, width), bf),
+            pltpu.VMEM((2, 3, hr, width), bf),
+            pltpu.VMEM((4, hr, 128), f32),
+            pltpu.VMEM((4, 3, hr, 128), f32),
+            dma((2, 2)), dma((chunks,)),
+            dma((RING,)), dma((2 * chunks,)), dma((RING,)), dma((2 * chunks,)),
+            dma((RING,)), dma((2 * chunks,)), dma((RING,)), dma((2 * chunks,)),
+            dma((2, 3)), dma((2, 3)), dma((2, 3)), dma((2, 3)), dma((4, 3)), dma((4, 3)),
+        ],
+        compiler_params=pltpu.CompilerParams(
+            collective_id=0, has_side_effects=True, vmem_limit_bytes=62 * 1024 * 1024
+        ),
+        cost_estimate=pl.CostEstimate(
+            flops=flops, bytes_accessed=10 * gate_weight.size, transcendentals=0
+        ),
+    )(activations, norm_gain[None, :], gate_weight, up_weight, down_weight)
 
 
 def solution(mesh):
@@ -62,6 +320,15 @@
         P("wid", "hid"),
         P("hid", "wid"),
     )
+
+    def body(activations, norm_gain, gate_weight, up_weight, down_weight):
+        fits = (
+            mesh.shape["wid"] == 4 and mesh.shape["hid"] == 4
+            and activations.shape == (64, 2048) and gate_weight.shape[1] == 14 * UNITS
+        )
+        form = kernel_body if fits else plain_body
+        return form(activations, norm_gain, gate_weight, up_weight, down_weight)
+
     return jax.shard_map(
         body, mesh=mesh, in_specs=placed, out_specs=P(("groups", "hid"), "wid"), check_vma=False
     )

time: 445 us -> 187 us (0.42)
  waiting for transfers between devices: 300 us -> 0 us
  Pallas kernels: 0 us -> 185 us
  matrix products: 92.2 us -> 0 us
  other arithmetic: 21.1 us -> 0 us
  blocking collectives: 13.7 us -> 0 us
  between operations: 13.6 us -> 0.01 us
    pallas_call x0 -> x1, Pallas kernels: none -> 185 us  [kernel_body(): pl.pallas_call(functools.partial(kernel, chunks), out_shape=jax.ShapeDtyp...]
    reduce_scatter x4 -> x0, waiting for transfers between devices: 181 us -> none  [the longest x2 130 us: combine_hidden(): lax.psum_scatter(partials.astype(jnp.bfloat16), 'wid', scatter_dimension=...]
    all_gather x4 -> x0, waiting for transfers between devices: 119 us -> none  [the longest x2 63.2 us: combine_hidden(): return lax.all_gather(hidden_share, 'wid', axis=1, tiled=True)]
    dot_general x6 -> x0, matrix products: 92.2 us -> none  [the longest x2 35.2 us: project_local(): up_part = jnp.dot(inputs, up_weight, preferred_element_type=jnp.float32)]
    psum x2 -> x0, blocking collectives: 13.7 us -> none  [normed(): total_sq = lax.psum(partial_sq, 'wid')]
    convert_element_type x7 -> x0, other arithmetic: 11.7 us -> none  [the longest x2 3.56 us: normed(): return (wide * factor[:, None] * norm_gain[None, :]).astype(jnp.bfloat16)]
    another operation x2 -> x0, other arithmetic: 7.14 us -> none  [project_local(): jnp.stack([gate_part, up_part]).astype(jnp.bfloat16).astype(jnp.float32)]
  transfers between devices with their start and end apart: 8 -> 0, of which waited for: 8 -> 0; matrix products, arithmetic and copies ran while one was open for 0% -> 0% of each run, Pallas kernels for 0% -> 0%
where the time goes in v1:
time: 187 us
  Pallas kernels  185 us (99%)
    pallas_call x1, Pallas kernels, kernel_body(): pl.pallas_call(functools.partial(kernel, chunks), out_shape=jax.ShapeDtyp...  185 us

profile of v1, /device:TPU:12, one launch (start us, length us, event | category | flops | bytes accessed | tf_op | source)
XLA Modules:
  0.0 186.8 jit_solution(15721339594518417658)
XLA Ops:
  0.0 185.1 %shard_map.55 = bf16[64,2048]{1,0:T(8,128)(2,1)} custom-call(bf16[64,2048]{1,0:T(8,128)(2,1)} %x_ref.1, f32[1,2048]{1,0:T(1,128)} %bitcast.1, bf16[2048,7168]{1,0:T(8,128)(2,1)} %wg_hbm.1, bf16[2048,7168]{1,0:T(8,128)(2,1)} %wu_hbm.1, bf16[7168,2048]{1,0:T(8,128)(2,1)} %wd_hbm.1), custom_call_target="tpu_custom_call" | custom-call | flops 45097156608 | bytes 146800640 | tf_op jit(solution)/shard_map/pallas_call | solution.py:281
  185.2 1.7 copy.7

commit v2 on v1

--- a/solution.py
+++ b/solution.py
@@ -12,6 +12,7 @@
 UNITS = 512
 LAG2, LAG3, LAG4, LAG5 = 1, 3, 5, 6
 LAG_ROWS, LAG_NORM = 4, 2
+GAP = 3
 RING = 8
 
 
@@ -143,8 +144,12 @@
     pl.semaphore_wait(barrier, 6)
     for half in (0, 1):
         send_stats(half, rows[half].astype(jnp.float32))
-    for half in (0, 1):
-        norm_rows(half, half)
+    norm_rows(0, 0)
+
+    def chunk_at(time):
+        step, inner = lax.div(time, 2 * chunks + GAP), lax.rem(time, 2 * chunks + GAP)
+        cc = step * (2 * chunks) + inner
+        return cc, (time >= 0) & (inner < 2 * chunks) & (cc < total)
 
     def stage_copies(cc):
         ring, both = lax.rem(cc, RING), lax.rem(cc, 2 * chunks)
@@ -160,16 +165,22 @@
         return ring, half, c, a, b, hid, pair
 
     def body(g, carry):
-        @pl.when(g < total)
-        def _():
-            ring, half, c, a, *_ = stage_copies(g)
-
-            @pl.when(g + 1 < total)
-            def _():
-                for copy in weight_copies(g + 1):
+        cc1, active1 = chunk_at(g)
+        cc2, active2 = chunk_at(g - LAG2)
+        cc3, active3 = chunk_at(g - LAG3)
+        cc4, active4 = chunk_at(g - LAG4)
+        cc5, active5 = chunk_at(g - LAG5)
+
+        @pl.when(active1)
+        def _():
+            ring, half, c, a, *_ = stage_copies(cc1)
+
+            @pl.when(cc1 + 1 < total)
+            def _():
+                for copy in weight_copies(cc1 + 1):
                     copy.start()
 
-            @pl.when(g < chunks)
+            @pl.when(cc1 < chunks)
             def _():
                 down_copy(c).start()
 
@@ -178,8 +189,12 @@
                 for d in (1, 2, 3):
                     gather_copy(half, d).wait()
 
-            slot = lax.rem(g, 2)
-            for copy in weight_copies(g):
+            @pl.when(cc1 == 0)
+            def _():
+                norm_rows(1, 1)
+
+            slot = lax.rem(cc1, 2)
+            for copy in weight_copies(cc1):
                 copy.wait()
             left = acts[half].reshape(4 * half_rows, width)
             for gu in (0, 1):
@@ -189,9 +204,9 @@
                     part[ring, b % 2, b // 2, gu] = product[b * half_rows:(b + 1) * half_rows]
             a.start()
 
-        @pl.when((g >= LAG2) & (g < total + LAG2))
-        def _():
-            ring, half, c, a, b, *_ = stage_copies(g - LAG2)
+        @pl.when(active2)
+        def _():
+            ring, half, c, a, b, *_ = stage_copies(cc2)
             a.wait()
             send_b[ring] = (
                 part[ring, core, 1 - chip].astype(jnp.float32)
@@ -199,9 +214,9 @@
             ).astype(jnp.bfloat16)
             b.start()
 
-        @pl.when((g >= LAG3) & (g < total + LAG3))
-        def _():
-            ring, half, c, a, b, hid, _ = stage_copies(g - LAG3)
+        @pl.when(active3)
+        def _():
+            ring, half, c, a, b, hid, _ = stage_copies(cc3)
             b.wait()
             sums = (
                 part[ring, core, chip].astype(jnp.float32)
@@ -211,18 +226,17 @@
             hidden[half, c, core, chip] = (gate / (1.0 + jnp.exp(-gate)) * up).astype(jnp.bfloat16)
             hid.start()
 
-        @pl.when((g >= LAG4) & (g < total + LAG4))
-        def _():
-            *_, hid, pair = stage_copies(g - LAG4)
+        @pl.when(active4)
+        def _():
+            *_, hid, pair = stage_copies(cc4)
             hid.wait()
             pair.start()
 
-        @pl.when((g >= LAG5) & (g < total + LAG5))
-        def _():
-            cc = g - LAG5
-            ring, half, c, *_, pair = stage_copies(cc)
-
-            @pl.when(cc < chunks)
+        @pl.when(active5)
+        def _():
+            ring, half, c, *_, pair = stage_copies(cc5)
+
+            @pl.when(cc5 < chunks)
             def _():
                 down_copy(c).wait()
 
@@ -245,7 +259,7 @@
 
         for q in range(4):
             half = q % 2
-            at = q * chunks + chunks - 1 + LAG5 + LAG_ROWS
+            at = q * chunks + (q // 2) * GAP + chunks - 1 + LAG5 + LAG_ROWS
 
             @pl.when(g == at)
             def _():
@@ -268,7 +282,7 @@
 
         return carry
 
-    lax.fori_loop(0, total + LAG5 + LAG_ROWS, body, 0)
+    lax.fori_loop(0, total + GAP + LAG5 + LAG_ROWS, body, 0)
 
 
 def kernel_body(activations, norm_gain, gate_weight, up_weight, down_weight):

time: 187 us -> 177 us (0.947)
  Pallas kernels: 185 us -> 175 us
    pallas_call x1, Pallas kernels: 185 us -> 175 us  [kernel_body(): pl.pallas_call(functools.partial(kernel, chunks), out_shape=jax.ShapeDtyp...]
where the time goes in v2:
time: 177 us; the launch traced here: 176 us
  Pallas kernels  175 us (99%)
    pallas_call x1, Pallas kernels, kernel_body(): pl.pallas_call(functools.partial(kernel, chunks), out_shape=jax.ShapeDtyp...  175 us

profile of v2, /device:TPU:12, one launch (start us, length us, event | category | flops | bytes accessed | tf_op | source)
XLA Modules:
  0.0 176.4 jit_solution(13505227596787009528)
XLA Ops:
  0.0 174.7 %shard_map.55 = bf16[64,2048]{1,0:T(8,128)(2,1)} custom-call(bf16[64,2048]{1,0:T(8,128)(2,1)} %x_ref.1, f32[1,2048]{1,0:T(1,128)} %bitcast.1, bf16[2048,7168]{1,0:T(8,128)(2,1)} %wg_hbm.1, bf16[2048,7168]{1,0:T(8,128)(2,1)} %wu_hbm.1, bf16[7168,2048]{1,0:T(8,128)(2,1)} %wd_hbm.1), custom_call_target="tpu_custom_call" | custom-call | flops 45097156608 | bytes 146800640 | tf_op jit(solution)/shard_map/pallas_call | solution.py:295
  174.7 1.7 copy.7
